TPU v7x, 512 devices: a whole 4x8x8 slice. The times are simulated.
512 devices in a mesh: area: 128 (over z, y, core), nrn: 4 (over x).
Axes of the slice: x: 4, y: 8, z: 8, core: 2. Of those that a mesh axis runs over, the one named last changes fastest.
Arguments:
- history: float32 [4, 65536, 128], P(None, ('area', 'nrn')), may hold values from -1 to 1
- drive: float32 [65536, 128], P(('area', 'nrn')), may hold values from -6 to 6
- leak: float32 [65536], P(('area', 'nrn')), may hold values from 0.1 to 0.9
- w_local: float32 [65536, 512], P(('area', 'nrn')), may hold values from -0.25 to 0.25
- w_long: float32 [65536, 4, 1152], P(('area', 'nrn')), may hold values from -0.1875 to 0.1875
- sender_rows: int32 [512, 128, 9], P(('area', 'nrn')), may hold values from 0 to 127
- delays: int32 [128, 128], P('area'), may hold values from 1 to 4
- area_sizes: int32 [128], P('area'), may hold values from 256 to 512, as said below
Outputs:
- rates: float32 [65536, 128], P(('area', 'nrn'))
Inputs may be any that keep to these rules, and one draw needn't show every extreme that they name: `area_sizes`: every area has at least half of its 512 slots live; some area has all of them live, some exactly half. `sender_rows`: indices may repeat.
All inputs are finite; a program needn't handle non-finite values.
Results may differ from a plain program's by a relative error of at most 0.0018.
Values may be sent and summed in bfloat16 or wider, within the bound.
A program may use at most 64 MiB of HBM per device.

v0:
```python
import jax
import jax.numpy as jnp
from jax import lax
from jax.sharding import PartitionSpec as P

STEPS = 6


def cut_along(x, dim, peers):
    lengths = x.shape
    pieces = x.reshape(*lengths[:dim], peers, lengths[dim] // peers, *lengths[dim + 1 :])
    return jnp.moveaxis(pieces, dim, 0)


def sum_at_owner(x, axis, dim):
    peers = lax.axis_size(axis)
    pieces = lax.all_to_all(cut_along(x, dim, peers), axis, 0, 0, tiled=True)
    return jnp.sum(pieces, axis=0)


def unround(values):
    return lax.optimization_barrier(values).astype(jnp.float32)


def local(history, drive, leak, w_local, w_long, sender_rows, delays, area_sizes):
    history_depth, block_rows, stimuli = history.shape
    nrn_count = lax.axis_size("nrn")
    area_count = sender_rows.shape[1]
    proj_count = sender_rows.shape[2]
    offsets = lax.axis_index("nrn") * block_rows + jnp.arange(block_rows, dtype=jnp.int32)
    active = (offsets < area_sizes[0]).astype(jnp.float32)[:, None]
    states = history * active[None]
    picked = ((delays[0] - 1)[:, None] * block_rows + sender_rows[0]).reshape(-1)
    grouped = lax.all_to_all(w_long, "nrn", split_axis=1, concat_axis=0, tiled=True).reshape(
        nrn_count * block_rows, -1
    )
    for iteration in range(STEPS):
        flat_states = states.reshape(history_depth * block_rows, stimuli)
        outgoing = flat_states[picked].astype(jnp.bfloat16).reshape(area_count, proj_count, stimuli)
        incoming = lax.all_to_all(outgoing, "area", split_axis=0, concat_axis=0, tiled=True)
        current = states[0].astype(jnp.bfloat16)
        local_all = lax.all_gather(current, "nrn", axis=0, tiled=True)
        sources = unround(incoming).reshape(-1, stimuli)
        long_term = sum_at_owner(
            jnp.dot(
                grouped,
                sources,
                precision=lax.Precision.HIGHEST,
                preferred_element_type=jnp.float32,
            ),
            "nrn",
            0,
        )
        inputs = (
            long_term
            + jnp.dot(
                w_local,
                unround(local_all),
                precision=lax.Precision.HIGHEST,
                preferred_element_type=jnp.float32,
            )
            + drive
        )
        updated = active * (states[0] + leak[:, None] * (jnp.tanh(inputs) - states[0]))
        states = jnp.concatenate([updated[None], states[:-1]], axis=0)
    return states[0]


def solution(mesh):
    placed = (
        P(None, ("area", "nrn"), None),
        P(("area", "nrn"), None),
        P(("area", "nrn")),
        P(("area", "nrn"), None),
        P(("area", "nrn"), None, None),
        P(("area", "nrn"), None, None),
        P("area", None),
        P("area"),
    )
    return jax.shard_map(
        local, mesh=mesh, in_specs=placed, out_specs=P(("area", "nrn"), None), check_vma=False
    )
```

profile of v0, /device:TPU:1, one launch (start us, length us, event | category | flops | bytes accessed | tf_op | source)
XLA Modules:
  0.0 352.0 jit_solution(10322337798542457753)
XLA Ops:
  1.7 0.8 copy.13
  2.7 1.0 broadcast_multiply_fusion
  3.8 2.5 gather_fusion
  6.3 0.9 convert_element_type.85
  7.2 18.4 %all-to-all-start = ((bf16[128,9,128]{2,1,0:T(8,128)(2,1)}), bf16[128,9,128]{2,1,0:T(8,128)(2,1)S(1)}, u32[]{:S(2)}, u32[]{:S(2)}) async-start(bf16[128,9,128]{2,1,0:T(8,128)(2,1)} %convert_element_type.85), calls=%async_computation | async-start | bytes 1048576 | tf_op jit(solution)/shard_map/all_to_all | solution.py:40
  25.7 1.6 copy.14
  27.3 19.0 %all-to-all-done = bf16[128,9,128]{2,1,0:T(8,128)(2,1)S(1)} async-done(((bf16[128,9,128]{2,1,0:T(8,128)(2,1)}), bf16[128,9,128]{2,1,0:T(8,128)(2,1)S(1)}, u32[]{:S(2)}, u32[]{:S(2)}) %all-to-all-start) | async-done | bytes 294944 | tf_op jit(solution)/shard_map/all_to_all | solution.py:40
  46.2 4.0 %all-to-all-start.1 = ((f32[128,4,1152]{2,0,1:T(8,128)}), f32[128,4,1152]{2,0,1:T(8,128)S(1)}, u32[]{:S(2)}, u32[]{:S(2)}) async-start(f32[128,4,1152]{2,0,1:T(8,128)} %copy.14), calls=%async_computation.1 | async-start | bytes 4718592 | tf_op jit(solution)/shard_map/all_to_all | solution.py:34
  50.9 0.9 reshape.130
  51.8 27.9 %all-to-all-done.1 = f32[128,4,1152]{2,0,1:T(8,128)S(1)} async-done(((f32[128,4,1152]{2,0,1:T(8,128)}), f32[128,4,1152]{2,0,1:T(8,128)S(1)}, u32[]{:S(2)}, u32[]{:S(2)}) %all-to-all-start.1) | async-done | bytes 2359328 | tf_op jit(solution)/shard_map/all_to_all | solution.py:34
  79.6 2.5 convolution_bitcast_fusion.5
  82.1 0.7 copy.58
  82.8 3.4 all-to-all-start.2
  86.2 10.8 %all_gather.18 = bf16[512,128]{1,0:T(8,128)(2,1)S(1)} all-gather(bf16[128,128]{1,0:T(8,128)(2,1)S(1)} %fusion.46), channel_id=1, replica_groups=mesh['area'=128,'nrn'=4] {'nrn'}, dimensions={0}, use_global_device_ids=true | all-gather | bytes 163840 | tf_op jit(solution)/shard_map/all_gather | solution.py:42
  98.1 2.9 gather_fusion.1
  101.1 29.5 %all_to_all.75 = bf16[128,9,128]{2,1,0:T(8,128)(2,1)} all-to-all(bf16[128,9,128]{2,1,0:T(8,128)(2,1)S(1)} %convert_element_type.88), channel_id=1, replica_groups=mesh['area'=128,'nrn'=4] {'area'}, dimensions={0} | all-to-all | bytes 589824 | tf_op jit(solution)/shard_map/all_to_all | solution.py:40
  130.7 1.2 reshape.134
  131.9 1.5 convolution_bitcast_fusion.4
  134.0 3.4 all-to-all-start.4
  137.5 10.9 %all_gather.19 = bf16[512,128]{1,0:T(8,128)(2,1)S(1)} all-gather(bf16[128,128]{1,0:T(8,128)(2,1)S(1)} %get-tuple-element.5), channel_id=1, replica_groups=mesh['area'=128,'nrn'=4] {'nrn'}, dimensions={0}, use_global_device_ids=true | all-gather | bytes 163840 | tf_op jit(solution)/shard_map/all_gather | solution.py:42
  149.5 2.9 gather_fusion.2
  152.5 28.8 %all_to_all.76 = bf16[128,9,128]{2,1,0:T(8,128)(2,1)} all-to-all(bf16[128,9,128]{2,1,0:T(8,128)(2,1)S(1)} %convert_element_type.91), channel_id=1, replica_groups=mesh['area'=128,'nrn'=4] {'area'}, dimensions={0} | all-to-all | bytes 589824 | tf_op jit(solution)/shard_map/all_to_all | solution.py:40
  181.3 1.2 reshape.137
  182.6 1.5 convolution_bitcast_fusion.3
  184.0 0.7 copy.56
  184.7 3.4 all-to-all-start.6
  188.1 10.9 %all_gather.20 = bf16[512,128]{1,0:T(8,128)(2,1)S(1)} all-gather(bf16[128,128]{1,0:T(8,128)(2,1)S(1)} %get-tuple-element.7), channel_id=1, replica_groups=mesh['area'=128,'nrn'=4] {'nrn'}, dimensions={0}, use_global_device_ids=true | all-gather | bytes 163840 | tf_op jit(solution)/shard_map/all_gather | solution.py:42
  200.2 2.9 gather_fusion.3
  203.2 28.8 %all_to_all.77 = bf16[128,9,128]{2,1,0:T(8,128)(2,1)} all-to-all(bf16[128,9,128]{2,1,0:T(8,128)(2,1)S(1)} %convert_element_type.94), channel_id=1, replica_groups=mesh['area'=128,'nrn'=4] {'area'}, dimensions={0} | all-to-all | bytes 589824 | tf_op jit(solution)/shard_map/all_to_all | solution.py:40
  232.0 1.2 reshape.140
  233.2 1.5 convolution_bitcast_fusion.2
  234.7 0.7 copy.55
  235.4 3.4 all-to-all-start.8
  238.8 10.9 %all_gather.21 = bf16[512,128]{1,0:T(8,128)(2,1)S(1)} all-gather(bf16[128,128]{1,0:T(8,128)(2,1)S(1)} %get-tuple-element.9), channel_id=1, replica_groups=mesh['area'=128,'nrn'=4] {'nrn'}, dimensions={0}, use_global_device_ids=true | all-gather | bytes 163840 | tf_op jit(solution)/shard_map/all_gather | solution.py:42
  250.9 2.9 gather_fusion.4
  253.9 28.8 %all_to_all.78 = bf16[128,9,128]{2,1,0:T(8,128)(2,1)} all-to-all(bf16[128,9,128]{2,1,0:T(8,128)(2,1)S(1)} %convert_element_type.97), channel_id=1, replica_groups=mesh['area'=128,'nrn'=4] {'area'}, dimensions={0} | all-to-all | bytes 589824 | tf_op jit(solution)/shard_map/all_to_all | solution.py:40
  282.7 1.2 reshape.143
  283.9 1.5 convolution_bitcast_fusion.1
  285.4 0.7 copy.54
  286.1 3.4 all-to-all-start.10
  289.5 10.9 %all_gather.22 = bf16[512,128]{1,0:T(8,128)(2,1)S(1)} all-gather(bf16[128,128]{1,0:T(8,128)(2,1)S(1)} %get-tuple-element.11), channel_id=1, replica_groups=mesh['area'=128,'nrn'=4] {'nrn'}, dimensions={0}, use_global_device_ids=true | all-gather | bytes 163840 | tf_op jit(solution)/shard_map/all_gather | solution.py:42
  301.5 2.9 gather_fusion.5
  304.6 28.7 %all_to_all.79 = bf16[128,9,128]{2,1,0:T(8,128)(2,1)} all-to-all(bf16[128,9,128]{2,1,0:T(8,128)(2,1)S(1)} %convert_element_type.100), channel_id=1, replica_groups=mesh['area'=128,'nrn'=4] {'area'}, dimensions={0} | all-to-all | bytes 589824 | tf_op jit(solution)/shard_map/all_to_all | solution.py:40
  333.3 1.2 reshape.146
  334.5 1.5 convolution_bitcast_fusion
  336.7 3.4 all-to-all-start.12
  340.1 10.9 %all_gather.23 = bf16[512,128]{1,0:T(8,128)(2,1)S(1)} all-gather(bf16[128,128]{1,0:T(8,128)(2,1)S(1)} %get-tuple-element.13), channel_id=1, replica_groups=mesh['area'=128,'nrn'=4] {'nrn'}, dimensions={0}, use_global_device_ids=true | all-gather | bytes 163840 | tf_op jit(solution)/shard_map/all_gather | solution.py:42
  351.1 0.9 fusion.41
  (92 shorter events, 9.1 us)
Async XLA Ops:
  0.0 97.1 %copy-start = (f32[128,512]{1,0:T(8,128)S(1)}, f32[128,512]{1,0:T(8,128)}, u32[]{:S(2)}) copy-start(f32[128,512]{1,0:T(8,128)} %param.11) | copy-start | bytes 786436
  3.8 21.9 %copy-start.1 = (f32[128,4,1152]{2,1,0:T(4,128)S(1)}, f32[128,4,1152]{2,1,0:T(4,128)}, u32[]{:S(2)}) copy-start(f32[128,4,1152]{2,1,0:T(4,128)} %param.12) | copy-start | bytes 7077892
  7.2 39.0 %all-to-all-start = ((bf16[128,9,128]{2,1,0:T(8,128)(2,1)}), bf16[128,9,128]{2,1,0:T(8,128)(2,1)S(1)}, u32[]{:S(2)}, u32[]{:S(2)}) async-start(bf16[128,9,128]{2,1,0:T(8,128)(2,1)} %convert_element_type.85), calls=%async_computation | async-start | bytes 1048576 | tf_op jit(solution)/shard_map/all_to_all | solution.py:40
  46.2 33.4 %all-to-all-start.1 = ((f32[128,4,1152]{2,0,1:T(8,128)}), f32[128,4,1152]{2,0,1:T(8,128)S(1)}, u32[]{:S(2)}, u32[]{:S(2)}) async-start(f32[128,4,1152]{2,0,1:T(8,128)} %copy.14), calls=%async_computation.1 | async-start | bytes 4718592 | tf_op jit(solution)/shard_map/all_to_all | solution.py:34
  51.8 45.4 %copy-start.2 = (f32[128,128]{1,0:T(8,128)S(1)}, f32[128,128]{1,0:T(8,128)}, u32[]{:S(2)}) copy-start(f32[128,128]{1,0:T(8,128)} %param.9) | copy-start | bytes 196612
  51.8 45.4 %copy-start.21 = (f32[128]{0:T(128)S(1)}, f32[128]{0:T(128)}, u32[]{:S(2)}) copy-start(f32[128]{0:T(128)} %param.10) | copy-start | bytes 1540
  79.6 17.8 %copy-start.11 = (bf16[3,128,128]{2,1,0:T(8,128)(2,1)S(1)}, bf16[3,128,128]{2,1,0:T(8,128)(2,1)}, u32[]{:S(2)}) copy-start(bf16[3,128,128]{2,1,0:T(8,128)(2,1)} %slice.39) | copy-start | bytes 294916
  82.8 14.2 %all-to-all-start.2 = ((f32[4,128,128]{1,2,0:T(8,128)}), f32[4,128,128]{1,2,0:T(8,128)S(1)}, u32[]{:S(2)}, u32[]{:S(2)}) async-start(f32[4,128,128]{1,2,0:T(8,128)} %bitcast.180), calls=%async_computation.2 | async-start | bytes 524288 | tf_op jit(solution)/shard_map/all_to_all | solution.py:17
  97.4 0.6 copy-start.3
  130.7 17.7 %copy-start.4 = (f32[128,128]{1,0:T(8,128)S(1)}, f32[128,128]{1,0:T(8,128)}, u32[]{:S(2)}) copy-start(f32[128,128]{1,0:T(8,128)} %copy-done.3) | copy-start | bytes 196612
  130.7 17.7 %copy-start.12 = (bf16[3,128,128]{2,1,0:T(8,128)(2,1)S(1)}, bf16[3,128,128]{2,1,0:T(8,128)(2,1)}, u32[]{:S(2)}) copy-start(bf16[3,128,128]{2,1,0:T(8,128)(2,1)} %slice.39) | copy-start | bytes 294916
  134.0 14.4 %all-to-all-start.4 = ((f32[4,128,128]{1,2,0:T(8,128)}), f32[4,128,128]{1,2,0:T(8,128)S(1)}, u32[]{:S(2)}, u32[]{:S(2)}) async-start(f32[4,128,128]{1,2,0:T(8,128)} %bitcast.179), calls=%async_computation.4 | async-start | bytes 524288 | tf_op jit(solution)/shard_map/all_to_all | solution.py:17
  148.4 0.6 copy-start.13
  148.8 0.6 copy-start.5
  181.3 17.8 %copy-start.6 = (f32[128,128]{1,0:T(8,128)S(1)}, f32[128,128]{1,0:T(8,128)}, u32[]{:S(2)}) copy-start(f32[128,128]{1,0:T(8,128)} %copy-done.5) | copy-start | bytes 196612
  181.3 17.8 %copy-start.14 = (bf16[3,128,128]{2,1,0:T(8,128)(2,1)S(1)}, bf16[3,128,128]{2,1,0:T(8,128)(2,1)}, u32[]{:S(2)}) copy-start(bf16[3,128,128]{2,1,0:T(8,128)(2,1)} %copy-done.13) | copy-start | bytes 294916
  184.7 14.4 %all-to-all-start.6 = ((f32[4,128,128]{1,2,0:T(8,128)}), f32[4,128,128]{1,2,0:T(8,128)S(1)}, u32[]{:S(2)}, u32[]{:S(2)}) async-start(f32[4,128,128]{1,2,0:T(8,128)} %bitcast.178), calls=%async_computation.6 | async-start | bytes 524288 | tf_op jit(solution)/shard_map/all_to_all | solution.py:17
  199.1 0.6 copy-start.15
  199.5 0.6 copy-start.7
  232.0 17.8 %copy-start.8 = (f32[128,128]{1,0:T(8,128)S(1)}, f32[128,128]{1,0:T(8,128)}, u32[]{:S(2)}) copy-start(f32[128,128]{1,0:T(8,128)} %copy-done.7) | copy-start | bytes 196612
  232.0 17.8 %copy-start.16 = (bf16[3,128,128]{2,1,0:T(8,128)(2,1)S(1)}, bf16[3,128,128]{2,1,0:T(8,128)(2,1)}, u32[]{:S(2)}) copy-start(bf16[3,128,128]{2,1,0:T(8,128)(2,1)} %copy-done.15) | copy-start | bytes 294916
  235.4 14.4 %all-to-all-start.8 = ((f32[4,128,128]{1,2,0:T(8,128)}), f32[4,128,128]{1,2,0:T(8,128)S(1)}, u32[]{:S(2)}, u32[]{:S(2)}) async-start(f32[4,128,128]{1,2,0:T(8,128)} %bitcast.177), calls=%async_computation.8 | async-start | bytes 524288 | tf_op jit(solution)/shard_map/all_to_all | solution.py:17
  249.8 0.6 copy-start.17
  250.2 0.6 copy-start.9
  282.7 17.8 %copy-start.10 = (f32[128,128]{1,0:T(8,128)S(1)}, f32[128,128]{1,0:T(8,128)}, u32[]{:S(2)}) copy-start(f32[128,128]{1,0:T(8,128)} %copy-done.9) | copy-start | bytes 196612
  282.7 17.8 %copy-start.18 = (bf16[3,128,128]{2,1,0:T(8,128)(2,1)S(1)}, bf16[3,128,128]{2,1,0:T(8,128)(2,1)}, u32[]{:S(2)}) copy-start(bf16[3,128,128]{2,1,0:T(8,128)(2,1)} %copy-done.17) | copy-start | bytes 294916
  286.1 14.4 %all-to-all-start.10 = ((f32[4,128,128]{1,2,0:T(8,128)}), f32[4,128,128]{1,2,0:T(8,128)S(1)}, u32[]{:S(2)}, u32[]{:S(2)}) async-start(f32[4,128,128]{1,2,0:T(8,128)} %bitcast.176), calls=%async_computation.10 | async-start | bytes 524288 | tf_op jit(solution)/shard_map/all_to_all | solution.py:17
  300.9 0.6 copy-start.19
  334.5 16.7 %copy-start.20 = (f32[128,128]{1,0:T(8,128)S(1)}, f32[128,128]{1,0:T(8,128)}, u32[]{:S(2)}) copy-start(f32[128,128]{1,0:T(8,128)} %copy-done.19) | copy-start | bytes 196612
  336.7 14.4 %all-to-all-start.12 = ((f32[4,128,128]{1,2,0:T(8,128)}), f32[4,128,128]{1,2,0:T(8,128)S(1)}, u32[]{:S(2)}, u32[]{:S(2)}) async-start(f32[4,128,128]{1,2,0:T(8,128)} %bitcast.175), calls=%async_computation.12 | async-start | bytes 524288 | tf_op jit(solution)/shard_map/all_to_all | solution.py:17
where the time goes:
time: 355 us; the launch traced here: 352 us
  blocking collectives  210 us (59%)
  waiting for transfers between devices  46.8 us (13%)
  starting transfers between devices  42.9 us (12%)
  local copies, waits for them, and re-layouts  37 us (10%)
  matrix products  12 us (3%)
    all_to_all x5, blocking collectives, local(): lax.all_to_all(outgoing, 'area', split_axis=0, concat_axis=0, tiled=True)  145 us
    all_gather x6, blocking collectives, local(): local_all = lax.all_gather(current, 'nrn', axis=0, tiled=True)  65.5 us
    all_to_all x1, waiting for transfers between devices, local(): lax.all_to_all(w_long, 'nrn', split_axis=1, concat_axis=0, tiled=True)  27.9 us
    all_to_all x6, starting transfers between devices, sum_at_owner(): pieces = lax.all_to_all(cut_along(x, dim, peers), axis, 0, 0, tiled=True)  20.4 us
    all_to_all x1, waiting for transfers between devices, local(): lax.all_to_all(outgoing, 'area', split_axis=0, concat_axis=0, tiled=True)  19 us
    all_to_all x1, starting transfers between devices, local(): lax.all_to_all(outgoing, 'area', split_axis=0, concat_axis=0, tiled=True)  18.4 us
    gather x6, local copies, waits for them, and re-layouts, local(): flat_states[picked].astype(jnp.bfloat16)  17.1 us
    dot_general x6, matrix products, local(): jnp.dot(grouped, sources, precision=lax.Precision.HIGHEST, preferred_elem...  9.74 us
  transfers between devices with their start and end apart: 8, of which 2 were waited for; matrix products, arithmetic and copies ran while one was open for 1% of the time, Pallas kernels for 0%

commit v1 on v0

v1 whole, which is shorter than its diff:
```python
import jax
import jax.numpy as jnp
import numpy as np
from jax import lax
from jax.experimental import pallas as pl
from jax.experimental.pallas import tpu as pltpu
from jax.sharding import PartitionSpec as P

STEPS = 6
SIDE = 8
PEERS = 4
DEPTH = 4
ROWS = 128
PROJ = 9
SLOTS = 10
MSG = SLOTS * SIDE
CODES = 2 * SIDE * SLOTS
LONG = 2 * SIDE * MSG
ORDER = (4, 3, 5, 2, 6, 1, 7)
MESH = pl.DeviceIdType.MESH
F32 = jnp.float32
BF16 = jnp.bfloat16
UNITS = 32767.0 / 0.25


def kernel(
    history, drive, leak, sizes, table, w, out,
    tables, held, pick, mixed, msg, got, wg, halves, part, parts, rate, mask, pace,
    table_send, table_recv, first_send, first_recv, w_send, w_recv,
    hop1_send, hop1_recv, hop2_send, hop2_recv, x_send, x_recv,
):
    area = lax.axis_index("area")
    x = lax.axis_index("nrn")
    c = area % 2
    y = (area // 2) % SIDE
    z = area // (2 * SIDE)
    p = z + (y - z) * c
    s = y + (z - y) * c
    p_stride = 2 * SIDE + (2 - 2 * SIDE) * c
    s_stride = 2 + (2 * SIDE - 2) * c

    def at(pp, ss, cc):
        return pp * p_stride + ss * s_stride + cc

    def remote(src, dst, send, recv, target_area, target_x):
        return pltpu.make_async_remote_copy(
            src_ref=src, dst_ref=dst, send_sem=send, recv_sem=recv,
            device_id=(target_area, target_x), device_id_type=MESH,
        )

    def arrive(ref, recv):
        remote(ref, ref, recv, recv, area, x).wait_recv()

    near = [(p + r) % SIDE for r in ORDER]
    far = [(s + r) % SIDE for r in ORDER]
    every = [(p + r) % SIDE for r in (0,) + ORDER]
    across = [(x + r) % PEERS for r in (2, 1, 3)]

    barrier = pltpu.get_barrier_semaphore()
    for pp in near:
        pl.semaphore_signal(barrier, inc=1, device_id=(at(pp, s, c), x), device_id_type=MESH)
    for ss in far:
        pl.semaphore_signal(barrier, inc=1, device_id=(at(p, ss, c), x), device_id_type=MESH)
    for pp in every:
        pl.semaphore_signal(barrier, inc=1, device_id=(at(pp, s, 1 - c), x), device_id_type=MESH)
    for i in across:
        pl.semaphore_signal(barrier, inc=1, device_id=(area, i), device_id_type=MESH)

    alive = (lax.broadcasted_iota(jnp.int32, (ROWS, ROWS), 0) + x * ROWS < sizes[0]).astype(F32)
    mask[...] = alive
    pace[...] = jnp.broadcast_to(leak[...], (ROWS, ROWS)).T
    rate[...] = history[0] * alive
    for i in range(DEPTH):
        held[p, DEPTH - 1 - i] = (history[i] * alive).astype(BF16)
    tables[p] = table[...]

    pl.semaphore_wait(barrier, 2 * len(near) + len(every) + len(across))

    def table_copy(pp):
        return remote(table, tables.at[p], table_send.at[pp], table_recv.at[p], at(pp, s, c), x)

    def first_copy(pp):
        ref = held.at[p, pl.ds(0, DEPTH)]
        return remote(ref, ref, first_send.at[pp], first_recv.at[p], at(pp, s, c), x)

    def w_copy(i):
        return remote(w.at[i], wg.at[x], w_send.at[i], w_recv.at[x], area, i)

    def hop1_copy(t, pp):
        ref = held.at[p, t + DEPTH - 1]
        return remote(ref, ref, hop1_send.at[t, pp], hop1_recv.at[t, p], at(pp, s, c), x)

    def hop2_copy(t, ss, cc):
        a = ss * 2 + cc
        return remote(
            msg.at[t, a], got.at[t, c * SIDE + s], hop2_send.at[t, a], hop2_recv.at[t, c * SIDE + s], at(p, ss, cc), x
        )

    def x_copy(t, i):
        return remote(part.at[t, i], parts.at[t, x], x_send.at[t, i], x_recv.at[t, x], area, i)

    def halve(i, block):
        units = block.astype(jnp.int32)
        high = (units + 128) >> 8
        halves[i, :ROWS] = high.astype(F32).astype(BF16)
        halves[i, ROWS:] = (units - (high << 8)).astype(F32).astype(BF16)

    def product(i, sources):
        both = jnp.dot(halves[i], sources, preferred_element_type=F32)
        return (both[:ROWS] * 256.0 + both[ROWS:]) * (1.0 / UNITS)

    targets = [(ss, cc) for ss in far for cc in (c, 1 - c)] + [(s, 1 - c)]

    for pp in near:
        table_copy(pp).start()
    for i in across:
        w_copy(i).start()
    for pp in near:
        first_copy(pp).start()

    for pp in every:
        if pp is not every[0]:
            arrive(tables.at[pp], table_recv.at[pp])
        row = tables[pp, pl.ds(p, 1), :]
        wanted = jnp.concatenate(
            [jnp.broadcast_to(row[:, h * ROWS : (h + 1) * ROWS], (ROWS, ROWS)).T for h in range(2)], axis=0
        )[:CODES]
        lane = lax.broadcasted_iota(jnp.int32, (CODES, ROWS), 1).astype(F32)
        for b in range(DEPTH):
            pick[pp, :, b * ROWS : (b + 1) * ROWS] = jnp.where(wanted == lane + float(b * ROWS), 1.0, 0.0).astype(BF16)

    halve(x, w[x])

    def step(t, is_first):
        for pp in near:
            if is_first:
                arrive(held.at[pp, pl.ds(0, DEPTH)], first_recv.at[pp])
            else:
                arrive(held.at[pp, t + DEPTH - 1], hop1_recv.at[t, pp])
        for src in range(SIDE):
            states = jnp.concatenate([held[src, t + DEPTH - 1 - b] for b in range(DEPTH)], axis=0)
            mixed[pl.ds(src, CODES, stride=SIDE), :] = jnp.dot(pick[src], states, preferred_element_type=F32)
        for a in range(2 * SIDE):
            msg[t, a] = mixed[a * MSG : (a + 1) * MSG, :].astype(BF16)
        for ss, cc in targets:
            hop2_copy(t, ss, cc).start()
        got[t, c * SIDE + s] = msg[t, s * 2 + c]
        if is_first:
            for i in across:
                arrive(wg.at[i], w_recv.at[i])
                halve(i, wg[i])
        for ss in far:
            arrive(got.at[t, c * SIDE + ss], hop2_recv.at[t, c * SIDE + ss])
        for pp in every:
            arrive(got.at[t, (1 - c) * SIDE + pp], hop2_recv.at[t, (1 - c) * SIDE + pp])
        sources = jnp.concatenate([got[t].reshape(LONG, ROWS), held[p, t + DEPTH - 1]], axis=0)
        for i in across:
            part[t, i] = product(i, sources).astype(BF16)
            x_copy(t, i).start()
        total = product(x, sources) + drive[...]
        for i in across:
            arrive(parts.at[t, i], x_recv.at[t, i])
            total += parts[t, i].astype(F32)
        old = rate[...]
        new = mask[...] * (old + pace[...] * (jnp.tanh(total) - old))
        return new

    def advance(t, is_first):
        new = step(t, is_first)
        rate[...] = new
        held[p, t + DEPTH] = new.astype(BF16)
        for pp in near:
            hop1_copy(t + 1, pp).start()
        for ss, cc in targets:
            hop2_copy(t, ss, cc).wait_send()
        for i in across:
            x_copy(t, i).wait_send()
        if is_first:
            for pp in near:
                table_copy(pp).wait_send()
                first_copy(pp).wait_send()
            for i in across:
                w_copy(i).wait_send()
        else:
            for pp in near:
                hop1_copy(t, pp).wait_send()

    advance(0, True)

    @pl.loop(1, STEPS - 1)
    def _(t):
        advance(t, False)

    last = STEPS - 1
    out[...] = step(last, False)
    for pp in near:
        hop1_copy(last, pp).wait_send()
    for ss, cc in targets:
        hop2_copy(last, ss, cc).wait_send()
    for i in across:
        x_copy(last, i).wait_send()


def place_of_columns():
    place = np.zeros((2 * SIDE * SIDE * PROJ,), np.int32)
    for zz in range(SIDE):
        for yy in range(SIDE):
            for cc in range(2):
                for q in range(PROJ):
                    mid, src = (yy, zz) if cc == 0 else (SIDE + zz, yy)
                    place[((zz * SIDE + yy) * 2 + cc) * PROJ + q] = mid * MSG + q * SIDE + src
    return place


def local(history, drive, leak, w_local, w_long, sender_rows, delays, area_sizes):
    c = lax.axis_index("area") % 2
    picked = (delays[0] - 1)[:, None] * ROWS + sender_rows[0]
    by_z = picked.reshape(SIDE, 2 * SIDE, PROJ)
    by_y = picked.reshape(SIDE, SIDE, 2, PROJ).transpose(1, 0, 2, 3).reshape(SIDE, 2 * SIDE, PROJ)
    table = jnp.where(c == 0, by_z, by_y)
    table = jnp.pad(table, ((0, 0), (0, 0), (0, SLOTS - PROJ)), constant_values=-1).reshape(SIDE, CODES)
    table = jnp.pad(table, ((0, 0), (0, 2 * ROWS - CODES)), constant_values=-1).astype(F32)

    place = jnp.asarray(place_of_columns())
    spread = (place[:, None] == jnp.arange(LONG, dtype=jnp.int32)[None, :]).astype(BF16)
    units = jnp.round(w_long * UNITS).astype(jnp.int32)
    high = (units + 128) >> 8
    low = units - (high << 8)
    move = lambda a: jnp.einsum("nkc,cd->knd", a.astype(BF16), spread, preferred_element_type=F32)
    long = (move(high) * 256.0 + move(low)).astype(jnp.int32)
    near = jnp.round(w_local * UNITS).astype(jnp.int32).reshape(ROWS, PEERS, ROWS).transpose(1, 0, 2)
    w = jnp.concatenate([long, near], axis=2).astype(jnp.int16)

    vmem = pl.BlockSpec(memory_space=pltpu.VMEM)
    dma = pltpu.SemaphoreType.DMA
    return pl.pallas_call(
        kernel,
        out_shape=jax.ShapeDtypeStruct((ROWS, ROWS), F32),
        in_specs=[vmem, vmem, vmem, pl.BlockSpec(memory_space=pltpu.SMEM), vmem, vmem],
        out_specs=vmem,
        scratch_shapes=[
            pltpu.VMEM((SIDE, SIDE, 2 * ROWS), F32),
            pltpu.VMEM((SIDE, DEPTH + STEPS, ROWS, ROWS), BF16),
            pltpu.VMEM((SIDE, CODES, DEPTH * ROWS), BF16),
            pltpu.VMEM((LONG, ROWS), F32),
            pltpu.VMEM((STEPS, 2 * SIDE, MSG, ROWS), BF16),
            pltpu.VMEM((STEPS, 2 * SIDE, MSG, ROWS), BF16),
            pltpu.VMEM((PEERS, ROWS, LONG + ROWS), jnp.int16),
            pltpu.VMEM((PEERS, 2 * ROWS, LONG + ROWS), BF16),
            pltpu.VMEM((STEPS, PEERS, ROWS, ROWS), BF16),
            pltpu.VMEM((STEPS, PEERS, ROWS, ROWS), BF16),
            pltpu.VMEM((ROWS, ROWS), F32),
            pltpu.VMEM((ROWS, ROWS), F32),
            pltpu.VMEM((ROWS, ROWS), F32),
            dma((SIDE,)), dma((SIDE,)), dma((SIDE,)), dma((SIDE,)), dma((PEERS,)), dma((PEERS,)),
            dma((STEPS, SIDE)), dma((STEPS, SIDE)), dma((STEPS, 2 * SIDE)), dma((STEPS, 2 * SIDE)),
            dma((STEPS, PEERS)), dma((STEPS, PEERS)),
        ],
        compiler_params=pltpu.CompilerParams(
            collective_id=0, has_side_effects=True, vmem_limit_bytes=48 * 1024 * 1024
        ),
        cost_estimate=pl.CostEstimate(flops=2 * 10**9, bytes_accessed=4 * 10**6, transcendentals=10**5),
    )(history, drive, leak.reshape(1, ROWS), area_sizes, table, w)


def solution(mesh):
    placed = (
        P(None, ("area", "nrn"), None),
        P(("area", "nrn"), None),
        P(("area", "nrn")),
        P(("area", "nrn"), None),
        P(("area", "nrn"), None, None),
        P(("area", "nrn"), None, None),
        P("area", None),
        P("area"),
    )
    return jax.shard_map(
        local, mesh=mesh, in_specs=placed, out_specs=P(("area", "nrn"), None), check_vma=False
    )
```

time: 355 us -> 145 us (0.41)
  blocking collectives: 210 us -> 0 us
  Pallas kernels: 0 us -> 133 us
  waiting for transfers between devices: 46.8 us -> 0 us
  starting transfers between devices: 42.9 us -> 0 us
  local copies, waits for them, and re-layouts: 37 us -> 2.39 us
  matrix products: 12 us -> 4.08 us
    all_to_all x5 -> x0, blocking collectives: 145 us -> none  [local(): lax.all_to_all(outgoing, 'area', split_axis=0, concat_axis=0, tiled=True)]
    pallas_call x0 -> x1, Pallas kernels: none -> 133 us  [local(): pl.pallas_call(kernel, out_shape=jax.ShapeDtypeStruct((ROWS, ROWS), F32),...]
    all_gather x6 -> x0, blocking collectives: 65.5 us -> none  [local(): local_all = lax.all_gather(current, 'nrn', axis=0, tiled=True)]
    all_to_all x8 -> x0, waiting for transfers between devices: 46.8 us -> none  [the longest x1 27.9 us: local(): lax.all_to_all(w_long, 'nrn', split_axis=1, concat_axis=0, tiled=True)]
    all_to_all x8 -> x0, starting transfers between devices: 42.9 us -> none  [the longest x6 20.4 us: sum_at_owner(): pieces = lax.all_to_all(cut_along(x, dim, peers), axis, 0, 0, tiled=True)]
    gather x6 -> x0, local copies, waits for them, and re-layouts: 17.1 us -> none  [local(): flat_states[picked].astype(jnp.bfloat16)]
    reshape x12 -> x3, local copies, waits for them, and re-layouts: 11.2 us -> 0.38 us  [the longest x1 0.17 us: local(): jnp.round(w_local * UNITS).astype(jnp.int32).reshape(ROWS, PEERS, ROWS)]
    dot_general x12 -> x2, matrix products: 12 us -> 4.08 us  [local(): jnp.einsum('nkc,cd->knd', a.astype(BF16), spread, preferred_element_type=...]
  transfers between devices with their start and end apart: 8 -> 0, of which waited for: 2 -> 0; matrix products, arithmetic and copies ran while one was open for 1% -> 0% of each run, Pallas kernels for 0% -> 0%
where the time goes in v1:
time: 145 us
  Pallas kernels  133 us (92%)
  other arithmetic  4.93 us (3%)
  matrix products  4.08 us (3%)
  local copies, waits for them, and re-layouts  2.39 us (2%)
    pallas_call x1, Pallas kernels, local(): pl.pallas_call(kernel, out_shape=jax.ShapeDtypeStruct((ROWS, ROWS), F32),...  133 us
    dot_general x2, matrix products, local(): jnp.einsum('nkc,cd->knd', a.astype(BF16), spread, preferred_element_type=...  4.08 us
    convert_element_type x1, other arithmetic, local(): a.astype(BF16)  3.25 us

profile of v1, /device:TPU:1, one launch (start us, length us, event | category | flops | bytes accessed | tf_op | source)
XLA Modules:
  0.0 144.9 jit_solution(9852424911602646647)
XLA Ops:
  0.0 0.7 fusion.25
  0.7 0.1 mul.40
  0.8 0.8 copy.34
  1.6 0.1 add_bitcast_fusion
  1.8 0.1 copy.36
  1.9 0.1 mul.39
  2.0 0.7 reduce.1
  2.7 0.1 squeeze.6
  2.8 0.1 copy.46
  2.9 0.1 reshape.46
  3.0 0.0 copy-start.4
  3.0 3.3 %fusion.22 = (bf16[128,4,1152]{2,1,0:T(4,128)(2,1)S(1)}, bf16[128,4,1152]{2,1,0:T(4,128)(2,1)S(1)}) fusion(f32[128,4,1152]{2,1,0:T(4,128)} %param.13), kind=kLoop, calls=%fused_computation.13 | loop fusion | flops 5308416 | bytes 4718592 | tf_op jit(solution)/shard_map/convert_element_type | solution.py:229
  6.3 0.0 copy-done.4
  6.3 2.0 %fusion.1 = f32[1280,128,4]{0,1,2:T(8,128)S(1)} fusion(s32[1152]{0:T(1024)S(1)} %copy-done.4, bf16[128,4,1152]{2,1,0:T(4,128)(2,1)S(1)} %get-tuple-element.6), kind=kOutput, calls=%fused_computation.2 | convolution fusion | flops 1511424000 | bytes 3805696 | tf_op jit(solution)/shard_map/nkc,cd->knd/dot_general | solution.py:229
  8.3 0.0 copy-start.3
  8.3 2.1 %fusion.19 = s16[4,128,1280]{2,1,0:T(8,128)(2,1)S(1)} fusion(f32[1280,128,4]{0,1,2:T(8,128)S(1)} %fusion.1, s32[1152]{0:T(1024)S(1)} %copy-done.4, bf16[128,4,1152]{2,1,0:T(4,128)(2,1)S(1)} %get-tuple-element.5), kind=kOutput, calls=%fused_computation.10 | convolution fusion | flops 1514045440 | bytes 5116416 | tf_op jit(solution)/shard_map/nkc,cd->knd/dot_general | solution.py:229
  10.4 0.0 copy-done.3
  10.4 0.0 copy-start
  10.4 0.0 copy-start.1
  10.4 0.0 copy-start.2
  10.4 0.1 copy.42
  10.6 0.2 copy.43
  10.8 0.1 pad_add_fusion.w
  11.6 0.0 copy-done
  11.6 0.0 copy-done.1
  11.6 0.0 copy-done.2
  11.6 132.7 %shard_map.91 = f32[128,128]{1,0:T(8,128)S(1)} custom-call(f32[4,128,128]{2,1,0:T(8,128)S(1)} %copy-done, f32[128,128]{1,0:T(8,128)S(1)} %copy-done.1, f32[1,128]{1,0:T(1,128)S(1)} %bitcast.27, s32[1]{0:T(128)S(6)} %copy.52.sizes, f32[8,256]{1,0:T(8,128)S(1)} %pad_convert_fusion.table, s16[4,128,1408]{2,1,0:T(8,128)(2,1)S(1)} %pad_add_fusion.w), custom_call_target="tpu_custom_call" | custom-call | flops 2000000000 | bytes 4000000 | tf_op jit(solution)/shard_map/pallas_call | solution.py:236
  144.3 0.6 copy.53
  (5 shorter events, 0.1 us)
Async XLA Ops:
  3.0 3.3 %copy-start.4 = (s32[1152]{0:T(1024)S(1)}, s32[1152]{0:T(1024)}, u32[]{:S(2)}) copy-start(s32[1152]{0:T(1024)} %constant.36.clone) | copy-start | bytes 13828
  8.3 2.1 %copy-start.3 = (f32[128,512]{1,0:T(8,128)S(1)}, f32[128,512]{1,0:T(8,128)}, u32[]{:S(2)}) copy-start(f32[128,512]{1,0:T(8,128)} %param.12) | copy-start | bytes 786436
  10.4 1.2 copy-start
  10.4 1.1 copy-start.1
  10.4 1.1 copy-start.2

commit v2 on v1

--- a/solution.py
+++ b/solution.py
@@ -14,8 +14,9 @@
 PROJ = 9
 SLOTS = 10
 MSG = SLOTS * SIDE
-CODES = 2 * SIDE * SLOTS
+CODES = 2 * SIDE * PROJ
 LONG = 2 * SIDE * MSG
+COLUMNS = 2 * SIDE * SIDE * PROJ
 ORDER = (4, 3, 5, 2, 6, 1, 7)
 MESH = pl.DeviceIdType.MESH
 F32 = jnp.float32
@@ -24,8 +25,9 @@
 
 
 def kernel(
-    history, drive, leak, sizes, table, w, out,
-    tables, held, pick, mixed, msg, got, wg, halves, part, parts, rate, mask, pace,
+    history, drive, leak, sizes, sender_rows, delays, w_local, w_long, spread, out,
+    codes, table, tables, held, pick, mixed, msg, got, early, early_in, raw, moves, rows_in, w, wg, halves, part, parts, rate, mask, pace,
+    load_sem, early_send, early_recv,
     table_send, table_recv, first_send, first_recv, w_send, w_recv,
     hop1_send, hop1_recv, hop2_send, hop2_recv, x_send, x_recv,
 ):
@@ -56,6 +58,11 @@
     every = [(p + r) % SIDE for r in (0,) + ORDER]
     across = [(x + r) % PEERS for r in (2, 1, 3)]
 
+    loads = [pltpu.make_async_copy(w_long, raw, load_sem.at[0]), pltpu.make_async_copy(spread, moves, load_sem.at[1]),
+             pltpu.make_async_copy(sender_rows, rows_in, load_sem.at[2])]
+    for load in loads:
+        load.start()
+
     barrier = pltpu.get_barrier_semaphore()
     for pp in near:
         pl.semaphore_signal(barrier, inc=1, device_id=(at(pp, s, c), x), device_id_type=MESH)
@@ -72,15 +79,22 @@
     rate[...] = history[0] * alive
     for i in range(DEPTH):
         held[p, DEPTH - 1 - i] = (history[i] * alive).astype(BF16)
-    tables[p] = table[...]
-
-    pl.semaphore_wait(barrier, 2 * len(near) + len(every) + len(across))
+
+    loads[2].wait()
+    lags = jnp.broadcast_to(delays[...].astype(F32), (ROWS, ROWS)).T
+    codes[...] = jnp.full((ROWS, ROWS), -1.0, F32)
+    codes[:, :PROJ] = (lags[:, :PROJ] - 1.0) * ROWS + rows_in[0].astype(F32)
+    for pp in range(SIDE):
+        for ss in range(SIDE):
+            table[pp, 2 * ss : 2 * ss + 2, :] = codes[pl.ds(at(pp, ss, 0), 2), :]
+    tables[p] = table[p]
+    mixed[...] = jnp.zeros(mixed.shape, F32)
 
     def table_copy(pp):
-        return remote(table, tables.at[p], table_send.at[pp], table_recv.at[p], at(pp, s, c), x)
+        return remote(table.at[pp], tables.at[p], table_send.at[pp], table_recv.at[p], at(pp, s, c), x)
 
     def first_copy(pp):
-        ref = held.at[p, pl.ds(0, DEPTH)]
+        ref = held.at[p, pl.ds(1, DEPTH - 1)]
         return remote(ref, ref, first_send.at[pp], first_recv.at[p], at(pp, s, c), x)
 
     def w_copy(i):
@@ -111,41 +125,84 @@
 
     targets = [(ss, cc) for ss in far for cc in (c, 1 - c)] + [(s, 1 - c)]
 
+    def early_copy(pp):
+        return remote(early.at[pp], early_in.at[p], early_send.at[pp], early_recv.at[p], at(pp, s, c), x)
+
+    lane = lax.broadcasted_iota(jnp.int32, (2 * SIDE, ROWS), 1).astype(F32)
+
+    def one_hot(wanted, index):
+        for q in range(PROJ):
+            column = jnp.broadcast_to(wanted[:, q : q + 1], (2 * SIDE, ROWS))
+            for b in range(DEPTH):
+                pick[index, q * 2 * SIDE : (q + 1) * 2 * SIDE, b * ROWS : (b + 1) * ROWS] = jnp.where(
+                    column == lane + float(b * ROWS), 1.0, 0.0
+                ).astype(BF16)
+
+    states = jnp.concatenate([held[p, DEPTH - 1 - b] for b in range(DEPTH)], axis=0)
+    for pp in range(SIDE):
+        one_hot(table[pp], pp)
+        early[pp] = jnp.dot(pick[pp], states, preferred_element_type=F32).astype(BF16)
+
+    loads[0].wait()
+    loads[1].wait()
+    def prepare(k):
+        units = jnp.round(raw[:, k, :] * UNITS).astype(jnp.int32)
+        high = (units + 128) >> 8
+        both = jnp.concatenate([high, units - (high << 8)], axis=0).astype(F32).astype(BF16)
+        moved = jnp.dot(both, moves[...], preferred_element_type=F32)
+        w[k, :, :LONG] = (moved[:ROWS] * 256.0 + moved[ROWS:]).astype(jnp.int32).astype(jnp.int16)
+        near_units = jnp.round(w_local[:, k * ROWS : (k + 1) * ROWS] * UNITS)
+        w[k, :, LONG:] = near_units.astype(jnp.int32).astype(jnp.int16)
+
+    def give(k):
+        @pl.when(k != x)
+        def _():
+            w_copy(k).start()
+
+    for k in range(PEERS // 2):
+        prepare(k)
+
+    pl.semaphore_wait(barrier, 2 * len(near) + len(every) + len(across))
+
+    for pp in near:
+        early_copy(pp).start()
+    for k in range(PEERS):
+        if k >= PEERS // 2:
+            prepare(k)
+        give(k)
     for pp in near:
         table_copy(pp).start()
-    for i in across:
-        w_copy(i).start()
-    for pp in near:
-        first_copy(pp).start()
-
-    for pp in every:
-        if pp is not every[0]:
-            arrive(tables.at[pp], table_recv.at[pp])
-        row = tables[pp, pl.ds(p, 1), :]
-        wanted = jnp.concatenate(
-            [jnp.broadcast_to(row[:, h * ROWS : (h + 1) * ROWS], (ROWS, ROWS)).T for h in range(2)], axis=0
-        )[:CODES]
-        lane = lax.broadcasted_iota(jnp.int32, (CODES, ROWS), 1).astype(F32)
-        for b in range(DEPTH):
-            pick[pp, :, b * ROWS : (b + 1) * ROWS] = jnp.where(wanted == lane + float(b * ROWS), 1.0, 0.0).astype(BF16)
-
-    halve(x, w[x])
-
-    def step(t, is_first):
-        for pp in near:
+
+    def step(t, is_first, is_second=False):
+        for pp in every:
             if is_first:
-                arrive(held.at[pp, pl.ds(0, DEPTH)], first_recv.at[pp])
+                if pp is not every[0]:
+                    arrive(early_in.at[pp], early_recv.at[pp])
+                    rows = early_in[pp].astype(F32)
+                else:
+                    rows = early[p].astype(F32)
             else:
-                arrive(held.at[pp, t + DEPTH - 1], hop1_recv.at[t, pp])
-        for src in range(SIDE):
-            states = jnp.concatenate([held[src, t + DEPTH - 1 - b] for b in range(DEPTH)], axis=0)
-            mixed[pl.ds(src, CODES, stride=SIDE), :] = jnp.dot(pick[src], states, preferred_element_type=F32)
+                if pp is not every[0]:
+                    if is_second:
+                        arrive(held.at[pp, pl.ds(1, DEPTH - 1)], first_recv.at[pp])
+                    arrive(held.at[pp, t + DEPTH - 1], hop1_recv.at[t, pp])
+                states = jnp.concatenate([held[pp, t + DEPTH - 1 - b] for b in range(DEPTH)], axis=0)
+                rows = jnp.dot(pick[pp], states, preferred_element_type=F32)
+            for q in range(PROJ):
+                mixed[pl.ds(q * SIDE + pp, 2 * SIDE, stride=MSG), :] = rows[q * 2 * SIDE : (q + 1) * 2 * SIDE]
         for a in range(2 * SIDE):
             msg[t, a] = mixed[a * MSG : (a + 1) * MSG, :].astype(BF16)
         for ss, cc in targets:
             hop2_copy(t, ss, cc).start()
         got[t, c * SIDE + s] = msg[t, s * 2 + c]
         if is_first:
+            for pp in near:
+                first_copy(pp).start()
+            for pp in every:
+                if pp is not every[0]:
+                    arrive(tables.at[pp], table_recv.at[pp])
+                one_hot(tables[pp], pp)
+            halve(x, w[x])
             for i in across:
                 arrive(wg.at[i], w_recv.at[i])
                 halve(i, wg[i])
@@ -165,8 +222,8 @@
         new = mask[...] * (old + pace[...] * (jnp.tanh(total) - old))
         return new
 
-    def advance(t, is_first):
-        new = step(t, is_first)
+    def advance(t, is_first, is_second=False):
+        new = step(t, is_first, is_second)
         rate[...] = new
         held[p, t + DEPTH] = new.astype(BF16)
         for pp in near:
@@ -178,16 +235,19 @@
         if is_first:
             for pp in near:
                 table_copy(pp).wait_send()
-                first_copy(pp).wait_send()
+                early_copy(pp).wait_send()
             for i in across:
                 w_copy(i).wait_send()
         else:
             for pp in near:
+                if is_second:
+                    first_copy(pp).wait_send()
                 hop1_copy(t, pp).wait_send()
 
     advance(0, True)
-
-    @pl.loop(1, STEPS - 1)
+    advance(1, False, True)
+
+    @pl.loop(2, STEPS - 1)
     def _(t):
         advance(t, False)
 
@@ -213,38 +273,30 @@
 
 
 def local(history, drive, leak, w_local, w_long, sender_rows, delays, area_sizes):
-    c = lax.axis_index("area") % 2
-    picked = (delays[0] - 1)[:, None] * ROWS + sender_rows[0]
-    by_z = picked.reshape(SIDE, 2 * SIDE, PROJ)
-    by_y = picked.reshape(SIDE, SIDE, 2, PROJ).transpose(1, 0, 2, 3).reshape(SIDE, 2 * SIDE, PROJ)
-    table = jnp.where(c == 0, by_z, by_y)
-    table = jnp.pad(table, ((0, 0), (0, 0), (0, SLOTS - PROJ)), constant_values=-1).reshape(SIDE, CODES)
-    table = jnp.pad(table, ((0, 0), (0, 2 * ROWS - CODES)), constant_values=-1).astype(F32)
-
-    place = jnp.asarray(place_of_columns())
-    spread = (place[:, None] == jnp.arange(LONG, dtype=jnp.int32)[None, :]).astype(BF16)
-    units = jnp.round(w_long * UNITS).astype(jnp.int32)
-    high = (units + 128) >> 8
-    low = units - (high << 8)
-    move = lambda a: jnp.einsum("nkc,cd->knd", a.astype(BF16), spread, preferred_element_type=F32)
-    long = (move(high) * 256.0 + move(low)).astype(jnp.int32)
-    near = jnp.round(w_local * UNITS).astype(jnp.int32).reshape(ROWS, PEERS, ROWS).transpose(1, 0, 2)
-    w = jnp.concatenate([long, near], axis=2).astype(jnp.int16)
-
+    spread = jnp.asarray(place_of_columns()[:, None] == np.arange(LONG)[None, :], BF16)
     vmem = pl.BlockSpec(memory_space=pltpu.VMEM)
+    hbm = pl.BlockSpec(memory_space=pl.ANY)
     dma = pltpu.SemaphoreType.DMA
     return pl.pallas_call(
         kernel,
         out_shape=jax.ShapeDtypeStruct((ROWS, ROWS), F32),
-        in_specs=[vmem, vmem, vmem, pl.BlockSpec(memory_space=pltpu.SMEM), vmem, vmem],
+        in_specs=[vmem, vmem, vmem, pl.BlockSpec(memory_space=pltpu.SMEM), hbm, vmem, vmem, hbm, hbm],
         out_specs=vmem,
         scratch_shapes=[
-            pltpu.VMEM((SIDE, SIDE, 2 * ROWS), F32),
+            pltpu.VMEM((ROWS, ROWS), F32),
+            pltpu.VMEM((SIDE, 2 * SIDE, ROWS), F32),
+            pltpu.VMEM((SIDE, 2 * SIDE, ROWS), F32),
             pltpu.VMEM((SIDE, DEPTH + STEPS, ROWS, ROWS), BF16),
             pltpu.VMEM((SIDE, CODES, DEPTH * ROWS), BF16),
             pltpu.VMEM((LONG, ROWS), F32),
             pltpu.VMEM((STEPS, 2 * SIDE, MSG, ROWS), BF16),
             pltpu.VMEM((STEPS, 2 * SIDE, MSG, ROWS), BF16),
+            pltpu.VMEM((SIDE, CODES, ROWS), BF16),
+            pltpu.VMEM((SIDE, CODES, ROWS), BF16),
+            pltpu.VMEM((ROWS, PEERS, COLUMNS), F32),
+            pltpu.VMEM((COLUMNS, LONG), BF16),
+            pltpu.VMEM((1, ROWS, PROJ), jnp.int32),
+            pltpu.VMEM((PEERS, ROWS, LONG + ROWS), jnp.int16),
             pltpu.VMEM((PEERS, ROWS, LONG + ROWS), jnp.int16),
             pltpu.VMEM((PEERS, 2 * ROWS, LONG + ROWS), BF16),
             pltpu.VMEM((STEPS, PEERS, ROWS, ROWS), BF16),
@@ -252,15 +304,15 @@
             pltpu.VMEM((ROWS, ROWS), F32),
             pltpu.VMEM((ROWS, ROWS), F32),
             pltpu.VMEM((ROWS, ROWS), F32),
-            dma((SIDE,)), dma((SIDE,)), dma((SIDE,)), dma((SIDE,)), dma((PEERS,)), dma((PEERS,)),
+            dma((3,)), dma((SIDE,)), dma((SIDE,)), dma((SIDE,)), dma((SIDE,)), dma((SIDE,)), dma((SIDE,)), dma((PEERS,)), dma((PEERS,)),
             dma((STEPS, SIDE)), dma((STEPS, SIDE)), dma((STEPS, 2 * SIDE)), dma((STEPS, 2 * SIDE)),
             dma((STEPS, PEERS)), dma((STEPS, PEERS)),
         ],
         compiler_params=pltpu.CompilerParams(
-            collective_id=0, has_side_effects=True, vmem_limit_bytes=48 * 1024 * 1024
+            collective_id=0, has_side_effects=True, vmem_limit_bytes=60 * 1024 * 1024
         ),
         cost_estimate=pl.CostEstimate(flops=2 * 10**9, bytes_accessed=4 * 10**6, transcendentals=10**5),
-    )(history, drive, leak.reshape(1, ROWS), area_sizes, table, w)
+    )(history, drive, leak.reshape(1, ROWS), area_sizes, sender_rows, delays, w_local, w_long, spread)
 
 
 def solution(mesh):

time: 145 us -> 140 us (0.966)
  other arithmetic: 4.93 us -> 0 us
  matrix products: 4.08 us -> 0 us
  Pallas kernels: 133 us -> 137 us
    dot_general x2 -> x0, matrix products: 4.08 us -> none  [local(): jnp.einsum('nkc,cd->knd', a.astype(BF16), spread, preferred_element_type=...]
    pallas_call x1, Pallas kernels: 133 us -> 137 us  [local(): pl.pallas_call(kernel, out_shape=jax.ShapeDtypeStruct((ROWS, ROWS), F32),...]
    convert_element_type x2 -> x0, other arithmetic: 3.26 us -> none  [the longest x1 3.25 us: local(): a.astype(BF16)]
where the time goes in v2:
time: 140 us
  Pallas kernels  137 us (98%)
  local copies, waits for them, and re-layouts  2.89 us (2%)
    pallas_call x1, Pallas kernels, local(): pl.pallas_call(kernel, out_shape=jax.ShapeDtypeStruct((ROWS, ROWS), F32),...  137 us
    unnamed x2, local copies, waits for them, and re-layouts  2.89 us

profile of v2, /device:TPU:1, one launch (start us, length us, event | category | flops | bytes accessed | tf_op | source)
XLA Modules:
  0.0 140.1 jit_solution(8931236525649343861)
XLA Ops:
  0.7 1.4 %copy.10.sender_rows = s32[1,128,9]{2,1,0:T(8,128)} copy(s32[1,128,9]{1,0,2:T(1,128)} %param.14) | data formatting | bytes 9216 | tf_op args[5]
  2.1 136.6 %shard_map.91 = f32[128,128]{1,0:T(8,128)} custom-call(f32[4,128,128]{2,1,0:T(8,128)} %history.1, f32[128,128]{1,0:T(8,128)} %drive.1, f32[1,128]{1,0:T(1,128)} %bitcast.1, s32[1]{0:T(128)S(6)} %copy.12.sizes, s32[1,128,9]{2,1,0:T(8,128)} %copy.10.sender_rows, s32[1,128]{1,0:T(1,128)} %delays.1, f32[128,512]{1,0:T(8,128)} %w_local.1, ...), custom_call_target="tpu_custom_call" | custom-call | flops 2000000000 | bytes 4000000 | tf_op jit(solution)/shard_map/pallas_call | solution.py:280
  138.6 1.5 %copy.13 = f32[128,128]{1,0:T(8,128)} copy(f32[128,128]{1,0:T(8,128)} %shard_map.91) | data formatting | bytes 131072

commit v3 on v2

--- a/solution.py
+++ b/solution.py
@@ -81,9 +81,10 @@
         held[p, DEPTH - 1 - i] = (history[i] * alive).astype(BF16)
 
     loads[2].wait()
-    lags = jnp.broadcast_to(delays[...].astype(F32), (ROWS, ROWS)).T
     codes[...] = jnp.full((ROWS, ROWS), -1.0, F32)
-    codes[:, :PROJ] = (lags[:, :PROJ] - 1.0) * ROWS + rows_in[0].astype(F32)
+    for q in range(PROJ):
+        codes[q : q + 1, :] = (delays[...].astype(F32) - 1.0) * ROWS + rows_in[q].astype(F32)
+    codes[...] = codes[...].T
     for pp in range(SIDE):
         for ss in range(SIDE):
             table[pp, 2 * ss : 2 * ss + 2, :] = codes[pl.ds(at(pp, ss, 0), 2), :]
@@ -203,15 +204,15 @@
                     arrive(tables.at[pp], table_recv.at[pp])
                 one_hot(tables[pp], pp)
             halve(x, w[x])
-            for i in across:
-                arrive(wg.at[i], w_recv.at[i])
-                halve(i, wg[i])
         for ss in far:
             arrive(got.at[t, c * SIDE + ss], hop2_recv.at[t, c * SIDE + ss])
         for pp in every:
             arrive(got.at[t, (1 - c) * SIDE + pp], hop2_recv.at[t, (1 - c) * SIDE + pp])
         sources = jnp.concatenate([got[t].reshape(LONG, ROWS), held[p, t + DEPTH - 1]], axis=0)
-        for i in across:
+        for i in across[1:] + across[:1] if is_first else across:
+            if is_first:
+                arrive(wg.at[i], w_recv.at[i])
+                halve(i, wg[i])
             part[t, i] = product(i, sources).astype(BF16)
             x_copy(t, i).start()
         total = product(x, sources) + drive[...]
@@ -295,7 +296,7 @@
             pltpu.VMEM((SIDE, CODES, ROWS), BF16),
             pltpu.VMEM((ROWS, PEERS, COLUMNS), F32),
             pltpu.VMEM((COLUMNS, LONG), BF16),
-            pltpu.VMEM((1, ROWS, PROJ), jnp.int32),
+            pltpu.VMEM((PROJ, 1, ROWS), jnp.int32),
             pltpu.VMEM((PEERS, ROWS, LONG + ROWS), jnp.int16),
             pltpu.VMEM((PEERS, ROWS, LONG + ROWS), jnp.int16),
             pltpu.VMEM((PEERS, 2 * ROWS, LONG + ROWS), BF16),
@@ -312,7 +313,7 @@
             collective_id=0, has_side_effects=True, vmem_limit_bytes=60 * 1024 * 1024
         ),
         cost_estimate=pl.CostEstimate(flops=2 * 10**9, bytes_accessed=4 * 10**6, transcendentals=10**5),
-    )(history, drive, leak.reshape(1, ROWS), area_sizes, sender_rows, delays, w_local, w_long, spread)
+    )(history, drive, leak.reshape(1, ROWS), area_sizes, sender_rows.transpose(2, 0, 1), delays, w_local, w_long, spread)
 
 
 def solution(mesh):

time: 140 us -> 139 us (level)
  local copies, waits for them, and re-layouts: 2.89 us -> 1.47 us
    unnamed x2 -> x1, local copies, waits for them, and re-layouts: 2.89 us -> 1.47 us
where the time goes in v3:
time: 139 us
  Pallas kernels  137 us (99%)
  local copies, waits for them, and re-layouts  1.47 us (1%)
    pallas_call x1, Pallas kernels, local(): pl.pallas_call(kernel, out_shape=jax.ShapeDtypeStruct((ROWS, ROWS), F32),...  137 us

profile of v3, /device:TPU:1, one launch (start us, length us, event | category | flops | bytes accessed | tf_op | source)
XLA Modules:
  0.0 139.0 jit_solution(13034300622639007964)
XLA Ops:
  0.7 136.9 %shard_map.91 = f32[128,128]{1,0:T(8,128)} custom-call(f32[4,128,128]{2,1,0:T(8,128)} %history.1, f32[128,128]{1,0:T(8,128)} %drive.1, f32[1,128]{1,0:T(1,128)} %bitcast.3, s32[1]{0:T(128)S(6)} %copy.11.sizes, s32[9,1,128]{2,1,0:T(1,128)} %bitcast.2, s32[1,128]{1,0:T(1,128)} %delays.1, f32[128,512]{1,0:T(8,128)} %w_local.1, f32[128,4,1152]{2,1,0:T(4,128)} %w_long.1, ...), custom_call_target="tpu_custom_call" | custom-call | flops 2000000000 | bytes 4000000 | tf_op jit(solution)/shard_map/pallas_call | solution.py:281
  137.5 1.5 %copy.12 = f32[128,128]{1,0:T(8,128)} copy(f32[128,128]{1,0:T(8,128)} %shard_map.91) | data formatting | bytes 131072

commit v4 on v3

--- a/solution.py
+++ b/solution.py
@@ -26,7 +26,7 @@
 
 def kernel(
     history, drive, leak, sizes, sender_rows, delays, w_local, w_long, spread, out,
-    codes, table, tables, held, pick, mixed, msg, got, early, early_in, raw, moves, rows_in, w, wg, halves, part, parts, rate, mask, pace,
+    codes, table, tables, held, pick, older, mixed, msg, got, early, early_in, raw, moves, rows_in, w, wg, halves, part, parts, rate, mask, pace,
     load_sem, early_send, early_recv,
     table_send, table_recv, first_send, first_recv, w_send, w_recv,
     hop1_send, hop1_recv, hop2_send, hop2_recv, x_send, x_recv,
@@ -174,7 +174,14 @@
     for pp in near:
         table_copy(pp).start()
 
-    def step(t, is_first, is_second=False):
+    def foresee(t, is_second):
+        for pp in every:
+            if is_second and pp is not every[0]:
+                arrive(held.at[pp, pl.ds(1, DEPTH - 1)], first_recv.at[pp])
+            states = jnp.concatenate([held[pp, t + DEPTH - 1 - b] for b in range(1, DEPTH)], axis=0)
+            older[pp] = jnp.dot(pick[pp, :, ROWS:], states, preferred_element_type=F32)
+
+    def step(t, is_first):
         for pp in every:
             if is_first:
                 if pp is not every[0]:
@@ -184,11 +191,10 @@
                     rows = early[p].astype(F32)
             else:
                 if pp is not every[0]:
-                    if is_second:
-                        arrive(held.at[pp, pl.ds(1, DEPTH - 1)], first_recv.at[pp])
                     arrive(held.at[pp, t + DEPTH - 1], hop1_recv.at[t, pp])
-                states = jnp.concatenate([held[pp, t + DEPTH - 1 - b] for b in range(DEPTH)], axis=0)
-                rows = jnp.dot(pick[pp], states, preferred_element_type=F32)
+                rows = older[pp] + jnp.dot(
+                    pick[pp, :, :ROWS], held[pp, t + DEPTH - 1], preferred_element_type=F32
+                )
             for q in range(PROJ):
                 mixed[pl.ds(q * SIDE + pp, 2 * SIDE, stride=MSG), :] = rows[q * 2 * SIDE : (q + 1) * 2 * SIDE]
         for a in range(2 * SIDE):
@@ -224,11 +230,12 @@
         return new
 
     def advance(t, is_first, is_second=False):
-        new = step(t, is_first, is_second)
+        new = step(t, is_first)
         rate[...] = new
         held[p, t + DEPTH] = new.astype(BF16)
         for pp in near:
             hop1_copy(t + 1, pp).start()
+        foresee(t + 1, is_first)
         for ss, cc in targets:
             hop2_copy(t, ss, cc).wait_send()
         for i in across:
@@ -289,6 +296,7 @@
             pltpu.VMEM((SIDE, 2 * SIDE, ROWS), F32),
             pltpu.VMEM((SIDE, DEPTH + STEPS, ROWS, ROWS), BF16),
             pltpu.VMEM((SIDE, CODES, DEPTH * ROWS), BF16),
+            pltpu.VMEM((SIDE, CODES, ROWS), F32),
             pltpu.VMEM((LONG, ROWS), F32),
             pltpu.VMEM((STEPS, 2 * SIDE, MSG, ROWS), BF16),
             pltpu.VMEM((STEPS, 2 * SIDE, MSG, ROWS), BF16),

time: 139 us -> 138 us (level)
  no operation moved by 1% of the time
where the time goes in v4:
time: 138 us
  Pallas kernels  136 us (99%)
  local copies, waits for them, and re-layouts  1.47 us (1%)
    pallas_call x1, Pallas kernels, local(): pl.pallas_call(kernel, out_shape=jax.ShapeDtypeStruct((ROWS, ROWS), F32),...  136 us

profile of v4, /device:TPU:1, one launch (start us, length us, event | category | flops | bytes accessed | tf_op | source)
XLA Modules:
  0.0 137.7 jit_solution(7384784615578021763)
XLA Ops:
  0.7 135.6 %shard_map.91 = f32[128,128]{1,0:T(8,128)} custom-call(f32[4,128,128]{2,1,0:T(8,128)} %history.1, f32[128,128]{1,0:T(8,128)} %drive.1, f32[1,128]{1,0:T(1,128)} %bitcast.3, s32[1]{0:T(128)S(6)} %copy.11.sizes, s32[9,1,128]{2,1,0:T(1,128)} %bitcast.2, s32[1,128]{1,0:T(1,128)} %delays.1, f32[128,512]{1,0:T(8,128)} %w_local.1, f32[128,4,1152]{2,1,0:T(4,128)} %w_long.1, ...), custom_call_target="tpu_custom_call" | custom-call | flops 2000000000 | bytes 4000000 | tf_op jit(solution)/shard_map/pallas_call | solution.py:288
  136.3 1.5 %copy.12 = f32[128,128]{1,0:T(8,128)} copy(f32[128,128]{1,0:T(8,128)} %shard_map.91) | data formatting | bytes 131072
